TPU v7x, 128 devices: a whole 4x4x4 slice. The times are simulated.
128 devices in a mesh: cluster: 8 (over z, x_hi), dp: 16 (over y, x_lo, core).
Axes of the slice: x: 4 (x_hi: 2, x_lo: 2; x = x_hi * 2 + x_lo), y: 4, z: 4, core: 2. Of those that a mesh axis runs over, the one named last changes fastest.
Arguments:
- documents: bfloat16 [32768, 1024], P('dp', 'cluster'), may hold values from -64 to 64
- centroids: bfloat16 [16384, 1024], P('cluster'), may hold values from -8 to 8
- domain_mass: float32 [32768, 256], P('dp'), may hold values from 0.01 to 10
Outputs:
- lift: float32 [16384, 256], P(('cluster', 'dp'))
- information: float32 [], replicated
All inputs are finite; a program needn't handle non-finite values.
Results may differ from a plain program's by a relative error of at most 0.0013.
Values may be sent and summed in bfloat16 or wider, within the bound.
A program may use at most 128 MiB of HBM per device.

v0:
```python
import math
import jax
import jax.numpy as jnp
from jax import lax
from jax.sharding import PartitionSpec as P

E = 1024


def shards(documents, centroids, domain_mass):
    scale = 3.0 / math.sqrt(E)
    doc_rows = documents.shape[0]
    local_k = centroids.shape[0]
    docs_total = doc_rows * lax.axis_size("dp")
    own_rows = local_k // lax.axis_size("dp")
    columns = centroids
    scores = (
        lax.dot_general(
            lax.all_gather(documents, "cluster", axis=1, tiled=True),
            columns,
            (((1,), (1,)), ((), ())),
            preferred_element_type=jnp.float32,
        )
        * scale
    )
    row_max = lax.pmax(jnp.max(scores, axis=1), "cluster")
    expo = jnp.exp(scores - row_max[:, None])
    row_total = lax.psum(jnp.sum(expo, axis=1), "cluster")
    assign = (expo / row_total[:, None]).astype(jnp.bfloat16)
    shares = (domain_mass / jnp.sum(domain_mass, axis=1, keepdims=True)).astype(jnp.bfloat16)
    columns = assign
    whole = lax.psum(
        lax.dot_general(
            columns, shares, (((0,), (0,)), ((), ())), preferred_element_type=jnp.float32
        ),
        "dp",
    )
    summed = lax.dynamic_slice_in_dim(whole, lax.axis_index("dp") * own_rows, own_rows, 0)
    joint = summed / docs_total
    cluster_mass = jnp.sum(joint, axis=1)
    domain_prior = lax.psum(jnp.sum(joint, axis=0), ("cluster", "dp"))
    lift = joint / (cluster_mass[:, None] * domain_prior[None, :])
    information = lax.psum(jnp.sum(joint * jnp.log(lift)), ("cluster", "dp"))
    return (lift, information)


def solution(mesh):
    return jax.shard_map(
        shards,
        mesh=mesh,
        in_specs=(P("dp", "cluster"), P("cluster", None), P("dp", None)),
        out_specs=(P(("cluster", "dp"), None), P()),
        check_vma=False,
    )
```

profile of v0, /device:TPU:1, one launch (start us, length us, event | category | flops | bytes accessed | tf_op | source)
XLA Modules:
  0.0 423.9 jit_solution(605599507388424641)
XLA Ops:
  7.2 0.0 all-gather.2.cloned.1.call-start
  7.2 0.7 all-gather.2.cloned.1.call-update
  7.9 0.0 all-reduce.2.cloned.1.call-start
  7.9 1.9 reduce_sum.46
  9.9 77.0 %all-gather.2.cloned.1.call-done = bf16[2048,1024]{1,0:T(8,128)(2,1)} async-done(((bf16[2048,128]{1,0:T(8,128)(2,1)}), bf16[2048,1024]{1,0:T(8,128)(2,1)}) %all-gather.2.cloned.1.call-update) | async-done | bytes 4194320 | tf_op jit(solution)/shard_map/all_gather | solution.py:19
  86.9 15.1 %multiply_reduce_fusion = (f32[2048]{0:T(1024)S(1)}, f32[2048,2048]{0,1:T(8,128)}) fusion(bf16[2048,1024]{1,0:T(8,128)(2,1)} %all-gather.2.cloned.1.call-done, bf16[2048,1024]{1,0:T(8,128)(2,1)} %param.4), kind=kOutput, calls=%fused_computation.2 | convolution fusion | flops 8598321152 | bytes 25174016 | tf_op jit(solution)/shard_map/dot_general | solution.py:18
  102.0 16.6 %pmax.7 = f32[2048]{0:T(1024)S(1)} all-reduce(f32[2048]{0:T(1024)S(1)} %get-tuple-element.6), channel_id=1, replica_groups=mesh['cluster'=8,'dp'=16] {'cluster'}, use_global_device_ids=true, to_apply=%region_1.0 | all-reduce | flops 2048 | bytes 16384 | tf_op jit(solution)/shard_map/pmax | solution.py:26
  118.6 0.0 copy-start
  118.6 8.7 %fusion = f32[2048]{0:T(1024)S(1)} fusion(f32[2048,2048]{0,1:T(8,128)} %get-tuple-element.7, f32[2048]{0:T(1024)S(1)} %pmax.7), kind=kLoop, calls=%fused_computation.3 | loop fusion | flops 12580864 | bytes 16793600 | tf_op jit(solution)/shard_map/reduce_sum | solution.py:28
  127.3 18.2 %psum.28 = f32[2048]{0:T(1024)S(1)} all-reduce(f32[2048]{0:T(1024)S(1)} %fusion), channel_id=1, replica_groups=mesh['cluster'=8,'dp'=16] {'cluster'}, use_global_device_ids=true, to_apply=%region_3.0 | all-reduce | flops 2048 | bytes 16384 | tf_op jit(solution)/shard_map/psum | solution.py:28
  145.5 0.0 copy-done
  145.5 9.1 %fusion.1 = f32[2048,256]{1,0:T(8,128)} fusion(f32[2048,2048]{0,1:T(8,128)} %get-tuple-element.7, f32[2048]{0:T(1024)S(1)} %psum.28, f32[2048]{0:T(1024)S(1)} %pmax.7, f32[2048,256]{1,0:T(8,128)S(1)} %copy-done, f32[2048]{0:T(1024)S(1)} %reduce_sum.46), kind=kOutput, calls=%fused_computation.4 | convolution fusion | flops 2165309440 | bytes 20996096 | tf_op jit(solution)/shard_map/dot_general | solution.py:33
  154.6 0.0 all-reduce.2.cloned.1.call-update
  154.7 129.3 %all-reduce.2.cloned.1.call-done = f32[2048,256]{1,0:T(8,128)} async-done(((f32[2048,256]{1,0:T(8,128)}), f32[2048,256]{1,0:T(8,128)}) %all-reduce.2.cloned.1.call-update) | async-done | bytes 2097168 | tf_op jit(solution)/shard_map/psum | solution.py:32
  283.9 1.0 fusion.4
  284.9 67.3 %psum.30 = f32[256]{0:T(256)S(1)} all-reduce(f32[256]{0:T(256)S(1)} %get-tuple-element.3), channel_id=1, replica_groups=mesh['cluster'=8,'dp'=16] {'cluster','dp'}, use_global_device_ids=true, to_apply=%region_8.0 | all-reduce | flops 256 | bytes 2048 | tf_op jit(solution)/shard_map/psum | solution.py:41
  352.2 2.3 multiply_reduce_fusion.1
  354.5 62.6 %psum.31 = f32[]{:T(128)} all-reduce(f32[]{:T(128)} %get-tuple-element.4), channel_id=1, replica_groups=mesh['cluster'=8,'dp'=16] {'cluster','dp'}, use_global_device_ids=true, to_apply=%region_10.0 | all-reduce | flops 1 | bytes 8 | tf_op jit(solution)/shard_map/psum | solution.py:43
Async XLA Ops:
  7.2 79.7 %all-gather.2.cloned.1.call-start = ((), (), s32[]{:S(2)}) async-start(), calls=%async_computation | async-start | bytes 4718592 | tf_op jit(solution)/shard_map/all_gather | solution.py:19
  7.9 276.0 %all-reduce.2.cloned.1.call-start = ((), (), s32[]{:S(2)}) async-start(), calls=%async_computation.1 | async-start | bytes 4194304 | tf_op jit(solution)/shard_map/psum | solution.py:32
  118.6 26.9 %copy-start = (f32[2048,256]{1,0:T(8,128)S(1)}, f32[2048,256]{1,0:T(8,128)}, u32[]{:S(2)}) copy-start(f32[2048,256]{1,0:T(8,128)} %param.5) | copy-start | bytes 6291460
Sparse Core Ops, SparseCore 0:
  10.2 76.6 all-gather.1
  154.8 129.0 all-reduce.1
where the time goes:
time: 424 us
  waiting for transfers between devices  207 us (49%)
  blocking collectives  165 us (39%)
  matrix products  24.2 us (6%)
  between operations  14.1 us (3%)
  other arithmetic  13.9 us (3%)
    psum x1, waiting for transfers between devices, shards(): lax.psum(lax.dot_general(columns, shares, (((0,), (0,)), ((), ())), prefe...  129 us
    all_gather x1, waiting for transfers between devices, shards(): lax.all_gather(documents, 'cluster', axis=1, tiled=True)  77 us
    psum x1, blocking collectives, shards(): domain_prior = lax.psum(jnp.sum(joint, axis=0), ('cluster', 'dp'))  67.3 us
    psum x1, blocking collectives, shards(): information = lax.psum(jnp.sum(joint * jnp.log(lift)), ('cluster', 'dp'))  62.6 us
    psum x1, blocking collectives, shards(): row_total = lax.psum(jnp.sum(expo, axis=1), 'cluster')  18.2 us
    pmax x1, blocking collectives, shards(): row_max = lax.pmax(jnp.max(scores, axis=1), 'cluster')  16.6 us
    dot_general x1, matrix products, shards(): lax.dot_general(lax.all_gather(documents, 'cluster', axis=1, tiled=True),...  15.1 us
    dot_general x1, matrix products, shards(): lax.dot_general(columns, shares, (((0,), (0,)), ((), ())), preferred_elem...  9.11 us
  transfers between devices with their start and end apart: 2, of which 2 were waited for; matrix products, arithmetic and copies ran while one was open for 0% of the time, Pallas kernels for 0%

commit v1 on v0

--- a/solution.py
+++ b/solution.py
@@ -1,3 +1,4 @@
+import functools
 import math
 import jax
 import jax.numpy as jnp
@@ -5,6 +6,14 @@
 from jax.sharding import PartitionSpec as P
 
 E = 1024
+
+
+def _unite_files(original, which_axis):
+    block_next = lax.all_gather(original, which_axis).sum(axis=0)
+    return block_next
+
+
+bring_inputs = functools.partial(_unite_files, which_axis="dp")
 
 
 def shards(documents, centroids, domain_mass):
@@ -29,11 +38,10 @@
     assign = (expo / row_total[:, None]).astype(jnp.bfloat16)
     shares = (domain_mass / jnp.sum(domain_mass, axis=1, keepdims=True)).astype(jnp.bfloat16)
     columns = assign
-    whole = lax.psum(
+    whole = bring_inputs(
         lax.dot_general(
             columns, shares, (((0,), (0,)), ((), ())), preferred_element_type=jnp.float32
-        ),
-        "dp",
+        )
     )
     summed = lax.dynamic_slice_in_dim(whole, lax.axis_index("dp") * own_rows, own_rows, 0)
     joint = summed / docs_total

time: 424 us -> 480 us (1.13)
  waiting for transfers between devices: 207 us -> 254 us
  other arithmetic: 13.9 us -> 24 us
    all_gather x0 -> x1, waiting for transfers between devices: none -> 176 us  [_unite_files(): block_next = lax.all_gather(original, which_axis).sum(axis=0)]
    psum x1 -> x0, waiting for transfers between devices: 129 us -> none  [shards(): lax.psum(lax.dot_general(columns, shares, (((0,), (0,)), ((), ())), prefe...]
    reduce_sum x0 -> x1, other arithmetic: none -> 12.1 us  [_unite_files(): block_next = lax.all_gather(original, which_axis).sum(axis=0)]
where the time goes in v1:
time: 480 us
  waiting for transfers between devices  254 us (53%)
  blocking collectives  163 us (34%)
  matrix products  24.2 us (5%)
  other arithmetic  24 us (5%)
  between operations  14.1 us (3%)
    all_gather x1, waiting for transfers between devices, _unite_files(): block_next = lax.all_gather(original, which_axis).sum(axis=0)  176 us
    all_gather x1, waiting for transfers between devices, shards(): lax.all_gather(documents, 'cluster', axis=1, tiled=True)  77 us
    psum x1, blocking collectives, shards(): domain_prior = lax.psum(jnp.sum(joint, axis=0), ('cluster', 'dp'))  65.9 us
    psum x1, blocking collectives, shards(): information = lax.psum(jnp.sum(joint * jnp.log(lift)), ('cluster', 'dp'))  62.6 us
    psum x1, blocking collectives, shards(): row_total = lax.psum(jnp.sum(expo, axis=1), 'cluster')  18.2 us
    pmax x1, blocking collectives, shards(): row_max = lax.pmax(jnp.max(scores, axis=1), 'cluster')  16.7 us
    dot_general x1, matrix products, shards(): lax.dot_general(lax.all_gather(documents, 'cluster', axis=1, tiled=True),...  15.1 us
    reduce_sum x1, other arithmetic, _unite_files(): block_next = lax.all_gather(original, which_axis).sum(axis=0)  12.1 us
  transfers between devices with their start and end apart: 2, of which 2 were waited for; matrix products, arithmetic and copies ran while one was open for 0% of the time, Pallas kernels for 0%

profile of v1, /device:TPU:1, one launch (start us, length us, event | category | flops | bytes accessed | tf_op | source)
XLA Modules:
  0.0 479.6 jit_solution(17093495844632664655)
XLA Ops:
  7.2 0.0 all-gather.4.cloned.1.call-start
  7.2 0.7 all-gather.4.cloned.1.call-update
  7.9 0.0 all-gather.6.cloned.1.call-start
  7.9 1.9 reduce_sum.55
  9.9 77.0 %all-gather.4.cloned.1.call-done = bf16[2048,1024]{1,0:T(8,128)(2,1)} async-done(((bf16[2048,128]{1,0:T(8,128)(2,1)}), bf16[2048,1024]{1,0:T(8,128)(2,1)}) %all-gather.4.cloned.1.call-update) | async-done | bytes 4194320 | tf_op jit(solution)/shard_map/all_gather | solution.py:28
  86.9 15.1 %multiply_reduce_fusion = (f32[2048]{0:T(1024)S(1)}, f32[2048,2048]{0,1:T(8,128)}) fusion(bf16[2048,1024]{1,0:T(8,128)(2,1)} %all-gather.4.cloned.1.call-done, bf16[2048,1024]{1,0:T(8,128)(2,1)} %param.4), kind=kOutput, calls=%fused_computation.2 | convolution fusion | flops 8598321152 | bytes 25174016 | tf_op jit(solution)/shard_map/dot_general | solution.py:27
  102.0 0.0 copy-start
  102.0 16.7 %pmax.7 = f32[2048]{0:T(1024)S(1)} all-reduce(f32[2048]{0:T(1024)S(1)} %get-tuple-element.6), channel_id=1, replica_groups=mesh['cluster'=8,'dp'=16] {'cluster'}, use_global_device_ids=true, to_apply=%region_1.0 | all-reduce | flops 2048 | bytes 16384 | tf_op jit(solution)/shard_map/pmax | solution.py:35
  118.7 8.6 %fusion = f32[2048]{0:T(1024)S(1)} fusion(f32[2048,2048]{0,1:T(8,128)} %get-tuple-element.7, f32[2048]{0:T(1024)S(1)} %pmax.7), kind=kLoop, calls=%fused_computation.3 | loop fusion | flops 12580864 | bytes 16793600 | tf_op jit(solution)/shard_map/reduce_sum | solution.py:37
  127.3 18.2 %psum.21 = f32[2048]{0:T(1024)S(1)} all-reduce(f32[2048]{0:T(1024)S(1)} %fusion), channel_id=1, replica_groups=mesh['cluster'=8,'dp'=16] {'cluster'}, use_global_device_ids=true, to_apply=%region_3.0 | all-reduce | flops 2048 | bytes 16384 | tf_op jit(solution)/shard_map/psum | solution.py:37
  145.5 0.0 copy-done
  145.5 9.1 %fusion.1 = f32[2048,256]{1,0:T(8,128)} fusion(f32[2048,2048]{0,1:T(8,128)} %get-tuple-element.7, f32[2048]{0:T(1024)S(1)} %psum.21, f32[2048]{0:T(1024)S(1)} %pmax.7, f32[2048,256]{1,0:T(8,128)S(1)} %copy-done, f32[2048]{0:T(1024)S(1)} %reduce_sum.55), kind=kOutput, calls=%fused_computation.4 | convolution fusion | flops 2165309440 | bytes 20996096 | tf_op jit(solution)/shard_map/dot_general | solution.py:42
  154.6 0.0 all-gather.6.cloned.1.call-update
  154.6 176.1 %all-gather.6.cloned.1.call-done = f32[32768,256]{1,0:T(8,128)} async-done(((f32[2048,256]{1,0:T(8,128)}), f32[32768,256]{1,0:T(8,128)}) %all-gather.6.cloned.1.call-update) | async-done | bytes 33554448 | tf_op jit(solution)/shard_map/all_gather | solution.py:12
  330.7 12.1 %reduce_sum.56 = f32[2048,256]{1,0:T(8,128)S(1)} reduce(f32[16,2048,256]{2,1,0:T(8,128)} %bitcast.3, f32[]{:T(128)} %constant.3.clone.1), dimensions={0}, to_apply=%region_5.0 | reduce | flops 7864320 | bytes 35651588 | tf_op jit(solution)/shard_map/reduce_sum | solution.py:12
  342.8 0.1 fusion.4
  342.9 65.9 %psum.22 = f32[256]{0:T(256)S(1)} all-reduce(f32[256]{0:T(256)S(1)} %get-tuple-element.3), channel_id=1, replica_groups=mesh['cluster'=8,'dp'=16] {'cluster','dp'}, use_global_device_ids=true, to_apply=%region_8.0 | all-reduce | flops 256 | bytes 2048 | tf_op jit(solution)/shard_map/psum | solution.py:49
  408.8 1.4 multiply_reduce_fusion.1
  410.1 62.6 %psum.23 = f32[]{:T(128)} all-reduce(f32[]{:T(128)} %get-tuple-element.4), channel_id=1, replica_groups=mesh['cluster'=8,'dp'=16] {'cluster','dp'}, use_global_device_ids=true, to_apply=%region_10.0 | all-reduce | flops 1 | bytes 8 | tf_op jit(solution)/shard_map/psum | solution.py:51
Async XLA Ops:
  7.2 79.7 %all-gather.4.cloned.1.call-start = ((), (), s32[]{:S(2)}) async-start(), calls=%async_computation | async-start | bytes 4718592 | tf_op jit(solution)/shard_map/all_gather | solution.py:28
  7.9 322.8 %all-gather.6.cloned.1.call-start = ((), (), s32[]{:S(2)}) async-start(), calls=%async_computation.1 | async-start | bytes 35651584 | tf_op jit(solution)/shard_map/all_gather | solution.py:12
  102.0 43.5 %copy-start = (f32[2048,256]{1,0:T(8,128)S(1)}, f32[2048,256]{1,0:T(8,128)}, u32[]{:S(2)}) copy-start(f32[2048,256]{1,0:T(8,128)} %param.5) | copy-start | bytes 6291460
Sparse Core Ops, SparseCore 0:
  10.2 76.6 all-gather.3
  154.7 175.9 all-gather.5
